TPU v7x, 32 devices: a whole 2x2x4 slice. The times are simulated.
32 devices in a mesh: row: 4 (over z), col: 8 (over y, x, core).
Axes of the slice: x: 2, y: 2, z: 4, core: 2. Of those that a mesh axis runs over, the one named last changes fastest.
Arguments:
- coeffs: float32 [4096, 4096], P('row', 'col'), may hold values from -6 to 6
- hamiltonian_tiles: float32 [8, 4, 512, 512], P('col'), may hold values from -0.125 to 0.125
- source_lists: int32 [8, 3], P('col'), may hold values from 0 to 7, as said below
- present: int32 [8, 4, 4, 4], P('col'), may hold values 0 or 1
Outputs:
- sigma_vector: float32 [4096, 4096], P('row', 'col')
Inputs may be any that keep to these rules, and one draw needn't show every extreme that they name: `source_lists`: each row names 3 different tiles, never its own; every tile is named by some row.
All inputs are finite; a program needn't handle non-finite values. No bound on the sum of `present` on one device may be relied on, other than what follows from the above.
Results may differ from a plain program's by a relative error of at most 0.0003.
Values sent between devices are 32-bit elements; how exact they have to be, the bound alone decides.
A program may use at most 192 MiB of HBM per device.

v0:
```python
import jax
import jax.numpy as jnp
from jax import lax
from jax.sharding import PartitionSpec as P


def expand_mask(present_tile, block_size):
    return jnp.repeat(jnp.repeat(present_tile, block_size, axis=-2), block_size, axis=-1)


def product(left, right):
    return jnp.dot(left, right, precision=lax.Precision.HIGHEST, preferred_element_type=jnp.float32)


def on_device(coeffs, hamiltonian_tiles, source_lists, present):
    row_count, tile_size = coeffs.shape
    tile_pair = row_count // tile_size
    block_size = tile_size // present.shape[-1]
    masked = hamiltonian_tiles[0] * expand_mask(present[0], block_size).astype(jnp.float32)
    listed = source_lists[0]
    own_product = product(coeffs, masked[0])
    carried = own_product
    piece = lax.all_gather(coeffs, "col", axis=1, tiled=True)
    start = jnp.int32(0)
    width = piece.shape[1]
    for listed_slot in range(listed.shape[0]):
        first_column = listed[listed_slot] * tile_size
        inside = (first_column >= start) & (first_column < start + width)
        offset = jnp.clip(first_column, 0, width - tile_size)
        weights = masked[listed_slot + 1]

        def take(current, offset=offset, weights=weights):
            return current + product(lax.dynamic_slice_in_dim(piece, offset, tile_size, 1), weights)

        carried = lax.cond(inside, take, lambda current: current, carried)
    stacked = carried.reshape(tile_pair, tile_size, tile_size)
    row_devices = lax.axis_size("row")
    col_devices = lax.axis_size("col")
    sliver = tile_size // col_devices
    initial_sweep = lax.all_to_all(stacked, "col", split_axis=1, concat_axis=1, tiled=True)
    second_pass = lax.all_to_all(initial_sweep, "row", split_axis=1, concat_axis=1, tiled=True)
    regroup = second_pass.reshape(tile_pair, row_devices, tile_pair, sliver, tile_size)
    regroup = jnp.transpose(regroup, (1, 0, 2, 3, 4)).reshape(
        row_devices * tile_pair, tile_pair, sliver, tile_size
    )
    third_pass = lax.all_to_all(regroup, "col", split_axis=0, concat_axis=0, tiled=True)
    mirrored = jnp.transpose(third_pass, (1, 3, 0, 2)).reshape(row_count, tile_size)
    return carried + mirrored


def solution(mesh):
    placed = (
        P("row", "col"),
        P("col", None, None, None),
        P("col", None),
        P("col", None, None, None),
    )
    return jax.shard_map(
        on_device, mesh=mesh, in_specs=placed, out_specs=P("row", "col"), check_vma=False
    )
```

profile of v0, /device:TPU:6, one launch (start us, length us, event | category | flops | bytes accessed | tf_op | source)
XLA Modules:
  0.0 250.1 jit_solution(4155500804595804740)
XLA Ops:
  6.5 0.7 all-gather.2.cloned.1.call-update
  7.3 0.7 fusion.24
  9.4 3.9 %broadcast_in_dim.7 = f32[4,512,4,128]{3,2,1,0:T(4,128)} broadcast(f32[4,512,4]{2,1,0:T(8,128)S(1)} %bitcast.40), dimensions={0,1,2} | broadcast | bytes 4227072 | tf_op jit(solution)/shard_map/broadcast_in_dim | solution.py:8
  13.2 5.5 %convert_element_type.37 = f32[4,512,512]{2,1,0:T(8,128)} reshape(f32[4,512,4,128]{3,2,1,0:T(4,128)} %broadcast_in_dim.7) | data formatting | bytes 8388608 | tf_op jit(solution)/shard_map/convert_element_type | solution.py:19
  18.7 5.8 %bitcast_multiply_fusion = f32[4,512,512]{2,1,0:T(8,128)S(1)} fusion(f32[4,512,512]{2,1,0:T(8,128)} %convert_element_type.37, f32[1,4,512,512]{3,2,1,0:T(8,128)} %param.11), kind=kLoop, calls=%fused_computation.18 | loop fusion | flops 1048576 | bytes 12582912 | tf_op jit(solution)/shard_map/mul | solution.py:19
  24.5 8.2 %convolution_bitcast_fusion = f32[1024,512]{0,1:T(8,128)} fusion(f32[1024,512]{1,0:T(8,128)S(1)} %copy-done.2, f32[4,512,512]{2,1,0:T(8,128)S(1)} %bitcast_multiply_fusion), kind=kOutput, calls=%fused_computation.19 | convolution fusion | flops 3221225472 | bytes 5242880 | tf_op jit(solution)/shard_map/dot_general | solution.py:12
  33.4 66.0 %all-gather.2.cloned.1.call-done = f32[1024,4096]{1,0:T(8,128)} async-done(((f32[1024,512]{1,0:T(8,128)}), f32[1024,4096]{1,0:T(8,128)}) %all-gather.2.cloned.1.call-update) | async-done | bytes 16777232 | tf_op jit(solution)/shard_map/all_gather | solution.py:23
  99.4 9.1 %conditional.3 = (f32[1024,512]{1,0:T(8,128)S(1)}) conditional(s32[]{:T(128)} %bitcast.7, (f32[1024,512]{0,1:T(8,128)}) %tuple.30, (s32[1,1]{1,0:T(1,128)}, f32[1024,4096]{1,0:T(8,128)}, f32[4,512,512]{2,1,0:T(8,128)}, f32[1024,512]{0,1:T(8,128)}, s32[1,1]{1,0:T(1,128)}, /*index=5*/s32[1,1]{1,0:T(1,128)}) %tuple.41), branch_computations={%region_0.1_spmd, %region_1.2_spmd} | conditional | flops 3221749760 | bytes 11534406 | solution.py:35
  99.4 2.9 %copy.19 = f32[1024,512]{1,0:T(8,128)} copy(f32[1024,512]{0,1:T(8,128)} %get-tuple-element.94) | data formatting | bytes 4194304 | tf_op jit(solution)/shard_map
  102.3 6.2 %fusion.2 = f32[1024,512]{1,0:T(8,128)S(1)} fusion(f32[1024,512]{1,0:T(8,128)} %copy.19, f32[1024,4096]{1,0:T(8,128)} %get-tuple-element.48, s32[]{:T(128)S(6)} %select_n.6, f32[4,512,512]{2,1,0:T(8,128)} %get-tuple-element.63), kind=kOutput, calls=%fused_computation.2 | convolution fusion | flops 3221749760 | bytes 7340036 | tf_op jit(solution)/shard_map/cond/branch_1_fun/dot_general | solution.py:12
  108.6 5.9 %conditional.4 = (f32[1024,512]{1,0:T(8,128)S(1)}) conditional(s32[]{:T(128)} %bitcast.6, f32[1024,512]{1,0:T(8,128)S(1)} %get-tuple-element.102, (s32[1,1]{1,0:T(1,128)}, f32[1024,4096]{1,0:T(8,128)}, f32[4,512,512]{2,1,0:T(8,128)}, f32[1024,512]{1,0:T(8,128)S(1)}, s32[1,1]{1,0:T(1,128)}, /*index=5*/s32[1,1]{1,0:T(1,128)}) %tuple.42), branch_computations={%region_2.3_spmd, %region_3.4_spmd} | conditional | flops 3221749760 | bytes 7340102 | solution.py:35
  108.6 5.9 %fusion.10 = f32[1024,512]{1,0:T(8,128)S(1)} fusion(f32[1024,512]{1,0:T(8,128)S(1)} %get-tuple-element.51, f32[1024,4096]{1,0:T(8,128)} %get-tuple-element.52, s32[]{:T(128)S(6)} %select_n.7, f32[4,512,512]{2,1,0:T(8,128)} %get-tuple-element.70), kind=kOutput, calls=%fused_computation.8 | convolution fusion | flops 3221749760 | bytes 7340036 | tf_op jit(solution)/shard_map/cond/branch_1_fun/dot_general | solution.py:12
  114.5 6.1 %conditional.5 = (f32[1024,512]{1,0:T(8,128)S(1)}) conditional(s32[]{:T(128)} %convert_element_type.29, f32[1024,512]{1,0:T(8,128)S(1)} %get-tuple-element.103, (s32[]{:T(128)}, f32[1024,4096]{1,0:T(8,128)}, f32[4,512,512]{2,1,0:T(8,128)}, f32[1024,512]{1,0:T(8,128)S(1)}) %tuple.43), branch_computations={%region_4.5_spmd, %region_5.6_spmd} | conditional | flops 3221749760 | bytes 7340068 | solution.py:35
  114.5 5.9 %fusion.18 = f32[1024,512]{1,0:T(8,128)S(1)} fusion(f32[1024,512]{1,0:T(8,128)S(1)} %get-tuple-element.55, f32[1024,4096]{1,0:T(8,128)} %get-tuple-element.56, s32[]{:T(128)S(6)} %min.12, f32[4,512,512]{2,1,0:T(8,128)} %get-tuple-element.58), kind=kOutput, calls=%fused_computation.14 | convolution fusion | flops 3221749760 | bytes 7340036 | tf_op jit(solution)/shard_map/cond/branch_1_fun/dot_general | solution.py:12
  120.6 1.6 copy.20
  122.2 28.2 %all_to_all.15 = f32[2,512,512]{2,0,1:T(2,128)S(1)} all-to-all(f32[2,512,512]{2,0,1:T(2,128)S(1)} %copy.20), channel_id=1, replica_groups=mesh['row'=4,'col'=8] {'col'}, dimensions={1} | all-to-all | bytes 4194304 | tf_op jit(solution)/shard_map/all_to_all | solution.py:40
  150.5 52.5 %all_to_all.16 = f32[2,512,512]{2,0,1:T(2,128)S(1)} all-to-all(f32[2,512,512]{2,0,1:T(2,128)S(1)} %all_to_all.15), channel_id=1, replica_groups=mesh['row'=4,'col'=8] {'row'}, dimensions={1} | all-to-all | bytes 4194304 | tf_op jit(solution)/shard_map/all_to_all | solution.py:41
  203.0 2.9 %copy.21 = f32[4,2,2,64,512]{4,2,3,1,0:T(2,128)} copy(f32[4,2,2,64,512]{4,1,3,2,0:T(2,128)S(1)} %bitcast.39) | data formatting | bytes 4194304 | tf_op jit(solution)/shard_map/transpose | solution.py:43
  206.0 6.1 %all-to-all-start.2 = ((f32[8,2,64,512]{3,1,2,0:T(2,128)}), f32[8,2,64,512]{3,1,2,0:T(2,128)}, u32[]{:S(2)}, u32[]{:S(2)}) async-start(f32[8,2,64,512]{3,1,2,0:T(2,128)} %bitcast.38), calls=%async_computation.2 | async-start | bytes 4194304 | tf_op jit(solution)/shard_map/all_to_all | solution.py:46
  212.0 1.8 copy.22
  213.8 22.6 %all-to-all-done.2 = f32[8,2,64,512]{3,1,2,0:T(2,128)} async-done(((f32[8,2,64,512]{3,1,2,0:T(2,128)}), f32[8,2,64,512]{3,1,2,0:T(2,128)}, u32[]{:S(2)}, u32[]{:S(2)}) %all-to-all-start.2) | async-done | bytes 2097184 | tf_op jit(solution)/shard_map/all_to_all | solution.py:46
  236.4 2.2 copy.25
  238.7 1.7 add.21
  240.4 2.9 %copy.23 = f32[1024,512]{1,0:T(8,128)} copy(f32[1024,512]{0,1:T(8,128)} %add.21) | data formatting | bytes 4194304 | tf_op jit(solution)/shard_map/add | solution.py:48
  (13 shorter events, 0.1 us)
Async XLA Ops:
  6.5 0.7 copy-start.4
  6.5 2.7 %copy-start.3 = (s32[1,4,4,4]{3,2,1,0:T(4,128)S(1)}, s32[1,4,4,4]{3,2,1,0:T(4,128)}, u32[]{:S(2)}) copy-start(s32[1,4,4,4]{3,2,1,0:T(4,128)} %param.13) | copy-start | bytes 772
  6.5 92.9 %all-gather.2.cloned.1.call-start = ((), (), s32[]{:S(2)}) async-start(), calls=%async_computation.3 | async-start | bytes 18874368 | tf_op jit(solution)/shard_map/all_gather | solution.py:23
  18.7 5.8 %copy-start.2 = (f32[1024,512]{1,0:T(8,128)S(1)}, f32[1024,512]{1,0:T(8,128)}, u32[]{:S(2)}) copy-start(f32[1024,512]{1,0:T(8,128)} %param.10) | copy-start | bytes 6291460
  24.5 8.2 %copy-start = (f32[4,512,512]{2,1,0:T(8,128)}, f32[4,512,512]{2,1,0:T(8,128)S(1)}, u32[]{:S(2)}) copy-start(f32[4,512,512]{2,1,0:T(8,128)S(1)} %bitcast_multiply_fusion) | copy-start | bytes 12582916
  206.0 30.5 %all-to-all-start.2 = ((f32[8,2,64,512]{3,1,2,0:T(2,128)}), f32[8,2,64,512]{3,1,2,0:T(2,128)}, u32[]{:S(2)}, u32[]{:S(2)}) async-start(f32[8,2,64,512]{3,1,2,0:T(2,128)} %bitcast.38), calls=%async_computation.2 | async-start | bytes 4194304 | tf_op jit(solution)/shard_map/all_to_all | solution.py:46
  236.4 2.2 copy-start.1
Sparse Core Ops, SparseCore 0:
  9.3 90.1 all-gather.1
where the time goes:
time: 254 us; the launch traced here: 250 us
  waiting for transfers between devices  89.4 us (35%)
  blocking collectives  80.8 us (32%)
  matrix products  26.2 us (10%)
  local copies, waits for them, and re-layouts  24.5 us (10%)
  between operations  15.5 us (6%)
  other arithmetic  7.5 us (3%)
  starting transfers between devices  6.07 us (2%)
    all_gather x1, waiting for transfers between devices, on_device(): piece = lax.all_gather(coeffs, 'col', axis=1, tiled=True)  66 us
    all_to_all x1, blocking collectives, on_device(): lax.all_to_all(initial_sweep, 'row', split_axis=1, concat_axis=1, tiled=T...  52.5 us
    all_to_all x1, blocking collectives, on_device(): lax.all_to_all(stacked, 'col', split_axis=1, concat_axis=1, tiled=True)  28.2 us
    dot_general x4, matrix products, product(): jnp.dot(left, right, precision=lax.Precision.HIGHEST, preferred_element_t...  26.2 us
    all_to_all x1, waiting for transfers between devices, on_device(): lax.all_to_all(regroup, 'col', split_axis=0, concat_axis=0, tiled=True)  22.6 us
    all_to_all x1, starting transfers between devices, on_device(): lax.all_to_all(regroup, 'col', split_axis=0, concat_axis=0, tiled=True)  6.06 us
    mul x1, other arithmetic, on_device(): hamiltonian_tiles[0]  5.76 us
    convert_element_type x1, local copies, waits for them, and re-layouts, on_device(): expand_mask(present[0], block_size).astype(jnp.float32)  5.49 us
  transfers between devices with their start and end apart: 2, of which 2 were waited for; matrix products, arithmetic and copies ran while one was open for 10% of the time, Pallas kernels for 0%

commit v1 on v0

v1 whole, which is shorter than its diff:
```python
import functools

import jax
import jax.numpy as jnp
from jax import lax
from jax.experimental import pallas as pl
from jax.experimental.pallas import tpu as pltpu
from jax.sharding import PartitionSpec as P

MESH = pl.DeviceIdType.MESH
AHEAD = 2


def kernel(sizes, source_ref, present_ref, c_ref, m_ref, out_ref, *scratch):
    row_devices, col_devices, chunks = sizes
    gathered = scratch[:chunks]
    high, low, half, mirror, g_send, g_recv, x_send, x_recv = scratch[chunks:]
    tile = c_ref.shape[1]
    pair = c_ref.shape[0] // tile
    rows = c_ref.shape[0] // chunks
    per_tile = tile // rows
    slots = m_ref.shape[1]
    blocks = present_ref.shape[2]
    block = tile // blocks
    r, c = lax.axis_index("row"), lax.axis_index("col")
    planes = col_devices // 4
    across = c ^ 2
    sibling = c ^ 1
    ups = [lax.rem(c + 4 * step, col_devices) for step in range(1, planes)]
    partners = [(c // pair, r * pair + u) for u in range(pair)]
    own_tile = lax.rem(c, pair)
    on_diagonal = c // pair == r

    barrier = pltpu.get_barrier_semaphore()
    for peer in [across, sibling] + ups:
        pl.semaphore_signal(barrier, inc=1, device_id=(r, peer), device_id_type=MESH)
    for u, partner in enumerate(partners):
        @pl.when(jnp.logical_not(on_diagonal & (own_tile == u)))
        def _(partner=partner):
            pl.semaphore_signal(barrier, inc=1, device_id=partner, device_id_type=MESH)
    expected = planes + 1 + pair
    pl.semaphore_wait(barrier, jnp.where(on_diagonal, expected - 1, expected))

    def where(k):
        return (k % pair) * tile + (k // pair) * rows

    sent = []
    counts = [0] * chunks

    def send(k, src, origin, target):
        copy = pltpu.make_async_remote_copy(
            src_ref=src, dst_ref=gathered[k].at[origin],
            send_sem=g_send.at[k, counts[k]], recv_sem=g_recv.at[k, origin],
            device_id=(r, target), device_id_type=MESH)
        counts[k] += 1
        copy.start()
        sent.append(copy)

    def arrived(k, origin):
        pltpu.make_async_remote_copy(
            src_ref=gathered[k].at[origin], dst_ref=gathered[k].at[origin],
            send_sem=g_send.at[k, 0], recv_sem=g_recv.at[k, origin],
            device_id=(r, sibling), device_id_type=MESH).wait_recv()

    def stage_own(k):
        mine = c_ref.at[pl.ds(where(k), rows)]
        send(k, mine, c, across)
        for up in ups:
            send(k, mine, c, up)
        send(k, mine, c, sibling)

    def stage_pass(k):
        arrived(k, across)
        if k % 2 == 0:
            for up in ups:
                send(k, gathered[k].at[across], across, up)
        send(k, gathered[k].at[across], across, sibling)
        for up in ups:
            arrived(k, up)
            if k % 2 == 1:
                send(k, gathered[k].at[up], up, across)
            send(k, gathered[k].at[up], up, sibling)

    def stage_far(k):
        for up in ups:
            arrived(k, up ^ 2)
            send(k, gathered[k].at[up ^ 2], up ^ 2, sibling)

    def exchange(u, j):
        span = pl.ds(j * rows, rows)
        return pltpu.make_async_remote_copy(
            src_ref=half.at[u, span], dst_ref=mirror.at[own_tile, span],
            send_sem=x_send.at[u, j], recv_sem=x_recv.at[own_tile, j],
            device_id=partners[u], device_id_type=MESH)

    def stage_multiply(k):
        arrived(k, sibling)
        arrived(k, sibling ^ 2)
        for up in ups:
            arrived(k, up ^ 1)
            arrived(k, up ^ 3)
        total = None
        for m in range(slots):
            x = c_ref[pl.ds(where(k), rows), :] if m == 0 else gathered[k][source_ref[0, m - 1]]
            x_high = x.astype(jnp.bfloat16)
            x_low = (x - x_high.astype(jnp.float32)).astype(jnp.bfloat16)
            for a, b in ((x_high, high), (x_low, high), (x_high, low)):
                term = jnp.dot(a, b[m], preferred_element_type=jnp.float32)
                total = term if total is None else total + term
        u, j = k % pair, k // pair
        span = pl.ds(j * rows, rows)
        half[u, span, :] = total
        local = on_diagonal & (own_tile == u)

        @pl.when(local)
        def _():
            mirror[u, span, :] = total

        @pl.when(jnp.logical_not(local))
        def _():
            exchange(u, j).start()

    for k in range(min(AHEAD, chunks)):
        stage_own(k)

    @pl.loop(0, slots)
    def _(m):
        for i in range(blocks):
            for j in range(blocks):
                place = (m, pl.ds(i * block, block), pl.ds(j * block, block))
                kept = m_ref[(0,) + place] * present_ref[0, m, i, j].astype(jnp.float32)
                top = kept.astype(jnp.bfloat16)
                high[place] = top
                low[place] = (kept - top.astype(jnp.float32)).astype(jnp.bfloat16)

    for step in range(chunks + 2):
        if step + AHEAD < chunks:
            stage_own(step + AHEAD)
        if step < chunks:
            stage_pass(step)
        if 0 <= step - 1 < chunks:
            stage_far(step - 1)
        if step >= 2:
            stage_multiply(step - 2)

    for j in range(per_tile):
        for u in range(pair):
            local = on_diagonal & (own_tile == u)
            span = pl.ds(j * rows, rows)

            @pl.when(jnp.logical_not(local))
            def _():
                pltpu.make_async_remote_copy(
                    src_ref=half.at[u, span], dst_ref=mirror.at[u, span],
                    send_sem=x_send.at[u, j], recv_sem=x_recv.at[u, j],
                    device_id=partners[u], device_id_type=MESH).wait_recv()

            out_ref[pl.ds(u * tile, tile), span] = half[u, :, span] + mirror[u, span, :].T

    for copy in sent:
        copy.wait_send()
    for j in range(per_tile):
        for u in range(pair):
            @pl.when(jnp.logical_not(on_diagonal & (own_tile == u)))
            def _():
                exchange(u, j).wait_send()


def on_device(row_devices, col_devices, coeffs, hamiltonian_tiles, source_lists, present):
    height, tile = coeffs.shape
    slots = hamiltonian_tiles.shape[1]
    pair = height // tile
    rows = min(tile, 128)
    chunks = height // rows
    planes = col_devices // 4
    sends = 4 * planes - 1
    return pl.pallas_call(
        functools.partial(kernel, (row_devices, col_devices, chunks)),
        out_shape=jax.ShapeDtypeStruct(coeffs.shape, jnp.float32),
        in_specs=[pl.BlockSpec(memory_space=pltpu.SMEM)] * 2
        + [pl.BlockSpec(memory_space=pltpu.VMEM)] * 2,
        out_specs=pl.BlockSpec(memory_space=pltpu.VMEM),
        scratch_shapes=[pltpu.VMEM((col_devices, rows, tile), jnp.float32) for _ in range(chunks)]
        + [
            pltpu.VMEM((slots, tile, tile), jnp.bfloat16),
            pltpu.VMEM((slots, tile, tile), jnp.bfloat16),
            pltpu.VMEM((pair, tile, tile), jnp.float32),
            pltpu.VMEM((pair, tile, tile), jnp.float32),
            pltpu.SemaphoreType.DMA((chunks, sends)),
            pltpu.SemaphoreType.DMA((chunks, col_devices)),
            pltpu.SemaphoreType.DMA((pair, tile // rows)),
            pltpu.SemaphoreType.DMA((pair, tile // rows)),
        ],
        compiler_params=pltpu.CompilerParams(
            collective_id=0, has_side_effects=True, vmem_limit_bytes=60 * 2**20),
    )(source_lists, present, coeffs, hamiltonian_tiles)


def solution(mesh):
    placed = (
        P("row", "col"),
        P("col", None, None, None),
        P("col", None),
        P("col", None, None, None),
    )
    body = functools.partial(on_device, mesh.shape["row"], mesh.shape["col"])
    return jax.shard_map(
        body, mesh=mesh, in_specs=placed, out_specs=P("row", "col"), check_vma=False
    )
```

time: 254 us -> 188 us (0.74)
  the two profiles are of different devices: /device:TPU:6 before, /device:TPU:29 now
where the time goes in v1:
time: 188 us
  Pallas kernels  185 us (98%)
  local copies, waits for them, and re-layouts  3.08 us (2%)
    pallas_call x1, Pallas kernels, on_device(): pl.pallas_call(functools.partial(kernel, (row_devices, col_devices, chunk...  185 us

profile of v1, /device:TPU:29, one launch (start us, length us, event | category | flops | bytes accessed | tf_op | source)
XLA Modules:
  0.0 187.7 jit_solution(17078540689973000077)
XLA Ops:
  0.0 184.6 %shard_map.46 = f32[1024,512]{1,0:T(8,128)} custom-call(s32[1,3]{1,0:T(1,128)} %source_ref.1, s32[1,4,4,4]{3,2,1,0:T(4,128)} %present_ref.1, f32[1024,512]{1,0:T(8,128)} %c_ref.1, f32[1,4,512,512]{3,2,1,0:T(8,128)} %m_ref.1), custom_call_target="tpu_custom_call" | custom-call | tf_op jit(solution)/shard_map/pallas_call | solution.py:177
  184.6 3.1 %copy.6 = f32[1024,512]{1,0:T(8,128)} copy(f32[1024,512]{1,0:T(8,128)} %shard_map.46) | data formatting | bytes 4194304

commit v2 on v1

--- a/solution.py
+++ b/solution.py
@@ -9,12 +9,14 @@
 
 MESH = pl.DeviceIdType.MESH
 AHEAD = 2
+DELAY = 1
 
 
 def kernel(sizes, source_ref, present_ref, c_ref, m_ref, out_ref, *scratch):
     row_devices, col_devices, chunks = sizes
     gathered = scratch[:chunks]
-    high, low, half, mirror, g_send, g_recv, x_send, x_recv = scratch[chunks:]
+    (high, low, half, mirror, first, second, g_send, g_recv, x_send, x_recv,
+     first_send, first_recv, second_send, second_recv) = scratch[chunks:]
     tile = c_ref.shape[1]
     pair = c_ref.shape[0] // tile
     rows = c_ref.shape[0] // chunks
@@ -27,19 +29,21 @@
     across = c ^ 2
     sibling = c ^ 1
     ups = [lax.rem(c + 4 * step, col_devices) for step in range(1, planes)]
-    partners = [(c // pair, r * pair + u) for u in range(pair)]
-    own_tile = lax.rem(c, pair)
-    on_diagonal = c // pair == r
+    chip, core = c // pair, lax.rem(c, pair)
+    apart = r ^ chip
+    lowest = apart & (0 - apart)
+    one_bit = (apart != 0) & (apart == lowest)
+    on_diagonal = apart == 0
 
     barrier = pltpu.get_barrier_semaphore()
-    for peer in [across, sibling] + ups:
+    for step in range(1, col_devices):
+        peer = lax.rem(c + step, col_devices)
         pl.semaphore_signal(barrier, inc=1, device_id=(r, peer), device_id_type=MESH)
-    for u, partner in enumerate(partners):
-        @pl.when(jnp.logical_not(on_diagonal & (own_tile == u)))
-        def _(partner=partner):
-            pl.semaphore_signal(barrier, inc=1, device_id=partner, device_id_type=MESH)
-    expected = planes + 1 + pair
-    pl.semaphore_wait(barrier, jnp.where(on_diagonal, expected - 1, expected))
+    for step in range(1, row_devices):
+        for other in range(pair):
+            peer = (lax.rem(r + step, row_devices), chip * pair + other)
+            pl.semaphore_signal(barrier, inc=1, device_id=peer, device_id_type=MESH)
+    pl.semaphore_wait(barrier, col_devices - 1 + pair * (row_devices - 1))
 
     def where(k):
         return (k % pair) * tile + (k // pair) * rows
@@ -86,12 +90,81 @@
             arrived(k, up ^ 2)
             send(k, gathered[k].at[up ^ 2], up ^ 2, sibling)
 
-    def exchange(u, j):
-        span = pl.ds(j * rows, rows)
-        return pltpu.make_async_remote_copy(
-            src_ref=half.at[u, span], dst_ref=mirror.at[own_tile, span],
-            send_sem=x_send.at[u, j], recv_sem=x_recv.at[own_tile, j],
-            device_id=partners[u], device_id_type=MESH)
+    def piece(j, route):
+        return pl.ds(j * rows + route * (rows // 2), rows // 2)
+
+    def source(u, j, route, act):
+        def go(dst, landed, target):
+            act(pltpu.make_async_remote_copy(
+                src_ref=half.at[u, piece(j, route)], dst_ref=dst,
+                send_sem=x_send.at[u, j, route], recv_sem=landed,
+                device_id=target, device_id_type=MESH))
+
+        @pl.when(on_diagonal & (core != u))
+        def _():
+            go(mirror.at[core, piece(j, route)], x_recv.at[core, j, route], (r, chip * pair + u))
+
+        bent = jnp.logical_not(on_diagonal) if route == 0 else jnp.logical_not(on_diagonal | one_bit)
+        via = chip ^ lowest if route == 0 else r ^ lowest
+
+        @pl.when(bent)
+        def _():
+            go(first.at[apart // 2, core, j], first_recv.at[apart // 2, core, j], (r, via * pair + u))
+
+        if route == 1:
+            @pl.when(one_bit)
+            def _():
+                go(second.at[apart // 2, core, j], second_recv.at[apart // 2, core, j],
+                   (chip, chip * pair + u))
+
+    def relay_first(j, forward):
+        for d in range(1, row_devices):
+            low_bit = d & -d
+            for route in range(2):
+                at = d ^ low_bit if route == 0 else low_bit
+                if at == d:
+                    continue
+
+                @pl.when(apart == at)
+                def _(d=d, route=route, at=at):
+                    for k in range(pair):
+                        landing = first.at[d // 2, k, j]
+                        if at == 0:
+                            dst, landed = mirror.at[k, piece(j, route)], x_recv.at[k, j, route]
+                        else:
+                            dst, landed = second.at[d // 2, k, j], second_recv.at[d // 2, k, j]
+                        forward(first_recv.at[d // 2, k, j], pltpu.make_async_remote_copy(
+                            src_ref=landing, dst_ref=dst, send_sem=first_send.at[d // 2, k, j],
+                            recv_sem=landed, device_id=(r ^ d, c), device_id_type=MESH), landing)
+
+    def relay_second(j, forward):
+        for d in range(1, row_devices):
+            low_bit = d & -d
+            for route in range(2):
+                at = low_bit if route == 0 else d ^ low_bit
+                if at == d:
+                    continue
+
+                @pl.when(apart == at)
+                def _(d=d, route=route):
+                    for k in range(pair):
+                        landing = second.at[d // 2, k, j]
+                        forward(second_recv.at[d // 2, k, j], pltpu.make_async_remote_copy(
+                            src_ref=landing, dst_ref=mirror.at[k, piece(j, route)],
+                            send_sem=second_send.at[d // 2, k, j], recv_sem=x_recv.at[k, j, route],
+                            device_id=(r, (r ^ d) * pair + core), device_id_type=MESH), landing)
+
+    def wait_landed(landed, ref):
+        pltpu.make_async_remote_copy(
+            src_ref=ref, dst_ref=ref, send_sem=x_send.at[0, 0, 0], recv_sem=landed,
+            device_id=(r, sibling), device_id_type=MESH).wait_recv()
+
+    def pass_on(landed, copy, landing):
+        wait_landed(landed, landing)
+        copy.start()
+
+    def finish(landed, copy, landing):
+        copy.wait_send()
 
     def stage_multiply(k):
         arrived(k, sibling)
@@ -110,15 +183,13 @@
         u, j = k % pair, k // pair
         span = pl.ds(j * rows, rows)
         half[u, span, :] = total
-        local = on_diagonal & (own_tile == u)
-
-        @pl.when(local)
+
+        @pl.when(on_diagonal & (core == u))
         def _():
             mirror[u, span, :] = total
 
-        @pl.when(jnp.logical_not(local))
-        def _():
-            exchange(u, j).start()
+        for route in range(2):
+            source(u, j, route, lambda copy: copy.start())
 
     for k in range(min(AHEAD, chunks)):
         stage_own(k)
@@ -133,27 +204,30 @@
                 high[place] = top
                 low[place] = (kept - top.astype(jnp.float32)).astype(jnp.bfloat16)
 
-    for step in range(chunks + 2):
+    for step in range(chunks + 2 + DELAY * 2):
         if step + AHEAD < chunks:
             stage_own(step + AHEAD)
         if step < chunks:
             stage_pass(step)
         if 0 <= step - 1 < chunks:
             stage_far(step - 1)
-        if step >= 2:
+        if 0 <= step - 2 < chunks:
             stage_multiply(step - 2)
+        done = step - 2 - DELAY
+        if done >= 0 and done % pair == pair - 1 and done // pair < per_tile:
+            relay_first(done // pair, pass_on)
+        done -= DELAY
+        if done >= 0 and done % pair == pair - 1 and done // pair < per_tile:
+            relay_second(done // pair, pass_on)
 
     for j in range(per_tile):
         for u in range(pair):
-            local = on_diagonal & (own_tile == u)
             span = pl.ds(j * rows, rows)
 
-            @pl.when(jnp.logical_not(local))
+            @pl.when(jnp.logical_not(on_diagonal & (core == u)))
             def _():
-                pltpu.make_async_remote_copy(
-                    src_ref=half.at[u, span], dst_ref=mirror.at[u, span],
-                    send_sem=x_send.at[u, j], recv_sem=x_recv.at[u, j],
-                    device_id=partners[u], device_id_type=MESH).wait_recv()
+                for route in range(2):
+                    wait_landed(x_recv.at[u, j, route], mirror.at[u, piece(j, route)])
 
             out_ref[pl.ds(u * tile, tile), span] = half[u, :, span] + mirror[u, span, :].T
 
@@ -161,9 +235,10 @@
         copy.wait_send()
     for j in range(per_tile):
         for u in range(pair):
-            @pl.when(jnp.logical_not(on_diagonal & (own_tile == u)))
-            def _():
-                exchange(u, j).wait_send()
+            for route in range(2):
+                source(u, j, route, lambda copy: copy.wait_send())
+        relay_first(j, finish)
+        relay_second(j, finish)
 
 
 def on_device(row_devices, col_devices, coeffs, hamiltonian_tiles, source_lists, present):
@@ -174,6 +249,7 @@
     chunks = height // rows
     planes = col_devices // 4
     sends = 4 * planes - 1
+    relayed = (row_devices // 2, pair, tile // rows)
     return pl.pallas_call(
         functools.partial(kernel, (row_devices, col_devices, chunks)),
         out_shape=jax.ShapeDtypeStruct(coeffs.shape, jnp.float32),
@@ -186,10 +262,16 @@
             pltpu.VMEM((slots, tile, tile), jnp.bfloat16),
             pltpu.VMEM((pair, tile, tile), jnp.float32),
             pltpu.VMEM((pair, tile, tile), jnp.float32),
+            pltpu.VMEM(relayed + (rows // 2, tile), jnp.float32),
+            pltpu.VMEM(relayed + (rows // 2, tile), jnp.float32),
             pltpu.SemaphoreType.DMA((chunks, sends)),
             pltpu.SemaphoreType.DMA((chunks, col_devices)),
-            pltpu.SemaphoreType.DMA((pair, tile // rows)),
-            pltpu.SemaphoreType.DMA((pair, tile // rows)),
+            pltpu.SemaphoreType.DMA((pair, tile // rows, 2)),
+            pltpu.SemaphoreType.DMA((pair, tile // rows, 2)),
+            pltpu.SemaphoreType.DMA(relayed),
+            pltpu.SemaphoreType.DMA(relayed),
+            pltpu.SemaphoreType.DMA(relayed),
+            pltpu.SemaphoreType.DMA(relayed),
         ],
         compiler_params=pltpu.CompilerParams(
             collective_id=0, has_side_effects=True, vmem_limit_bytes=60 * 2**20),

time: 188 us -> 123 us (0.65)
  the two profiles are of different devices: /device:TPU:29 before, /device:TPU:6 now
where the time goes in v2:
time: 123 us
  Pallas kernels  120 us (98%)
  local copies, waits for them, and re-layouts  3.08 us (3%)
    pallas_call x1, Pallas kernels, on_device(): pl.pallas_call(functools.partial(kernel, (row_devices, col_devices, chunk...  120 us
    unnamed x1, local copies, waits for them, and re-layouts  3.08 us

profile of v2, /device:TPU:6, one launch (start us, length us, event | category | flops | bytes accessed | tf_op | source)
XLA Modules:
  0.0 122.9 jit_solution(2214987260712647632)
XLA Ops:
  0.0 119.8 %shard_map.46 = f32[1024,512]{1,0:T(8,128)} custom-call(s32[1,3]{1,0:T(1,128)} %source_ref.1, s32[1,4,4,4]{3,2,1,0:T(4,128)} %present_ref.1, f32[1024,512]{1,0:T(8,128)} %c_ref.1, f32[1,4,512,512]{3,2,1,0:T(8,128)} %m_ref.1), custom_call_target="tpu_custom_call" | custom-call | tf_op jit(solution)/shard_map/pallas_call | solution.py:253
  119.8 3.1 %copy.6 = f32[1024,512]{1,0:T(8,128)} copy(f32[1024,512]{1,0:T(8,128)} %shard_map.46) | data formatting | bytes 4194304

commit v3 on v2

--- a/solution.py
+++ b/solution.py
@@ -10,18 +10,20 @@
 MESH = pl.DeviceIdType.MESH
 AHEAD = 2
 DELAY = 1
-
-
-def kernel(sizes, source_ref, present_ref, c_ref, m_ref, out_ref, *scratch):
-    row_devices, col_devices, chunks = sizes
+LAST = 2
+
+
+def kernel(sizes, source_ref, present_ref, c_hbm, m_hbm, out_hbm, *scratch):
+    row_devices, col_devices, segments = sizes
+    tile = c_hbm.shape[1]
+    pair = c_hbm.shape[0] // tile
+    chunks = pair * len(segments)
+    per_tile = len(segments)
     gathered = scratch[:chunks]
     (high, low, half, mirror, first, second, g_send, g_recv, x_send, x_recv,
-     first_send, first_recv, second_send, second_recv) = scratch[chunks:]
-    tile = c_ref.shape[1]
-    pair = c_ref.shape[0] // tile
-    rows = c_ref.shape[0] // chunks
-    per_tile = tile // rows
-    slots = m_ref.shape[1]
+     first_send, first_recv, second_send, second_recv,
+     c_ref, m_ref, out_ref, c_done, m_done, out_done) = scratch[chunks:]
+    slots = m_hbm.shape[1]
     blocks = present_ref.shape[2]
     block = tile // blocks
     r, c = lax.axis_index("row"), lax.axis_index("col")
@@ -35,6 +37,15 @@
     one_bit = (apart != 0) & (apart == lowest)
     on_diagonal = apart == 0
 
+    c_copy = pltpu.make_async_copy(c_hbm, c_ref, c_done)
+    c_copy.start()
+
+    def m_copy(m):
+        return pltpu.make_async_copy(m_hbm.at[0, m], m_ref.at[m], m_done.at[m])
+
+    for m in range(slots):
+        m_copy(m).start()
+
     barrier = pltpu.get_barrier_semaphore()
     for step in range(1, col_devices):
         peer = lax.rem(c + step, col_devices)
@@ -46,7 +57,8 @@
     pl.semaphore_wait(barrier, col_devices - 1 + pair * (row_devices - 1))
 
     def where(k):
-        return (k % pair) * tile + (k // pair) * rows
+        first_row, rows = segments[k // pair]
+        return pl.ds((k % pair) * tile + first_row, rows)
 
     sent = []
     counts = [0] * chunks
@@ -67,7 +79,7 @@
             device_id=(r, sibling), device_id_type=MESH).wait_recv()
 
     def stage_own(k):
-        mine = c_ref.at[pl.ds(where(k), rows)]
+        mine = c_hbm.at[where(k)]
         send(k, mine, c, across)
         for up in ups:
             send(k, mine, c, up)
@@ -91,7 +103,12 @@
             send(k, gathered[k].at[up ^ 2], up ^ 2, sibling)
 
     def piece(j, route):
-        return pl.ds(j * rows + route * (rows // 2), rows // 2)
+        first_row, rows = segments[j]
+        return pl.ds(first_row + route * (rows // 2), rows // 2)
+
+    def relayed(j):
+        first_row, rows = segments[j]
+        return pl.ds(first_row // 2, rows // 2)
 
     def source(u, j, route, act):
         def go(dst, landed, target):
@@ -109,12 +126,12 @@
 
         @pl.when(bent)
         def _():
-            go(first.at[apart // 2, core, j], first_recv.at[apart // 2, core, j], (r, via * pair + u))
+            go(first.at[apart // 2, core, relayed(j)], first_recv.at[apart // 2, core, j], (r, via * pair + u))
 
         if route == 1:
             @pl.when(one_bit)
             def _():
-                go(second.at[apart // 2, core, j], second_recv.at[apart // 2, core, j],
+                go(second.at[apart // 2, core, relayed(j)], second_recv.at[apart // 2, core, j],
                    (chip, chip * pair + u))
 
     def relay_first(j, forward):
@@ -128,11 +145,11 @@
                 @pl.when(apart == at)
                 def _(d=d, route=route, at=at):
                     for k in range(pair):
-                        landing = first.at[d // 2, k, j]
+                        landing = first.at[d // 2, k, relayed(j)]
                         if at == 0:
                             dst, landed = mirror.at[k, piece(j, route)], x_recv.at[k, j, route]
                         else:
-                            dst, landed = second.at[d // 2, k, j], second_recv.at[d // 2, k, j]
+                            dst, landed = second.at[d // 2, k, relayed(j)], second_recv.at[d // 2, k, j]
                         forward(first_recv.at[d // 2, k, j], pltpu.make_async_remote_copy(
                             src_ref=landing, dst_ref=dst, send_sem=first_send.at[d // 2, k, j],
                             recv_sem=landed, device_id=(r ^ d, c), device_id_type=MESH), landing)
@@ -148,7 +165,7 @@
                 @pl.when(apart == at)
                 def _(d=d, route=route):
                     for k in range(pair):
-                        landing = second.at[d // 2, k, j]
+                        landing = second.at[d // 2, k, relayed(j)]
                         forward(second_recv.at[d // 2, k, j], pltpu.make_async_remote_copy(
                             src_ref=landing, dst_ref=mirror.at[k, piece(j, route)],
                             send_sem=second_send.at[d // 2, k, j], recv_sem=x_recv.at[k, j, route],
@@ -172,16 +189,19 @@
         for up in ups:
             arrived(k, up ^ 1)
             arrived(k, up ^ 3)
+        rows = segments[k // pair][1]
         total = None
         for m in range(slots):
-            x = c_ref[pl.ds(where(k), rows), :] if m == 0 else gathered[k][source_ref[0, m - 1]]
+            x = c_ref[where(k), :] if m == 0 else gathered[k][source_ref[0, m - 1]]
             x_high = x.astype(jnp.bfloat16)
             x_low = (x - x_high.astype(jnp.float32)).astype(jnp.bfloat16)
-            for a, b in ((x_high, high), (x_low, high), (x_high, low)):
-                term = jnp.dot(a, b[m], preferred_element_type=jnp.float32)
-                total = term if total is None else total + term
+            both = jnp.dot(jnp.concatenate([x_high, x_low], axis=0), high[m],
+                           preferred_element_type=jnp.float32)
+            term = both[:rows] + both[rows:] + jnp.dot(
+                x_high, low[m], preferred_element_type=jnp.float32)
+            total = term if total is None else total + term
         u, j = k % pair, k // pair
-        span = pl.ds(j * rows, rows)
+        span = pl.ds(*segments[j])
         half[u, span, :] = total
 
         @pl.when(on_diagonal & (core == u))
@@ -196,14 +216,16 @@
 
     @pl.loop(0, slots)
     def _(m):
+        m_copy(m).wait()
         for i in range(blocks):
             for j in range(blocks):
                 place = (m, pl.ds(i * block, block), pl.ds(j * block, block))
-                kept = m_ref[(0,) + place] * present_ref[0, m, i, j].astype(jnp.float32)
+                kept = m_ref[place] * present_ref[0, m, i, j].astype(jnp.float32)
                 top = kept.astype(jnp.bfloat16)
                 high[place] = top
                 low[place] = (kept - top.astype(jnp.float32)).astype(jnp.bfloat16)
 
+    c_copy.wait()
     for step in range(chunks + 2 + DELAY * 2):
         if step + AHEAD < chunks:
             stage_own(step + AHEAD)
@@ -220,17 +242,27 @@
         if done >= 0 and done % pair == pair - 1 and done // pair < per_tile:
             relay_second(done // pair, pass_on)
 
-    for j in range(per_tile):
+    written = []
+    for first_row in range(0, tile, block):
         for u in range(pair):
-            span = pl.ds(j * rows, rows)
+            span = pl.ds(first_row, block)
 
             @pl.when(jnp.logical_not(on_diagonal & (core == u)))
             def _():
-                for route in range(2):
-                    wait_landed(x_recv.at[u, j, route], mirror.at[u, piece(j, route)])
-
-            out_ref[pl.ds(u * tile, tile), span] = half[u, :, span] + mirror[u, span, :].T
-
+                for j in range(per_tile):
+                    if first_row <= segments[j][0] < first_row + block:
+                        for route in range(2):
+                            wait_landed(x_recv.at[u, j, route], mirror.at[u, piece(j, route)])
+
+            place = (pl.ds(u * tile, tile), span)
+            out_ref[place] = half[u, :, span] + mirror[u, span, :].T
+            copy = pltpu.make_async_copy(
+                out_ref.at[place], out_hbm.at[place], out_done.at[u, first_row // block])
+            copy.start()
+            written.append(copy)
+
+    for copy in written:
+        copy.wait()
     for copy in sent:
         copy.wait_send()
     for j in range(per_tile):
@@ -245,33 +277,46 @@
     height, tile = coeffs.shape
     slots = hamiltonian_tiles.shape[1]
     pair = height // tile
-    rows = min(tile, 128)
-    chunks = height // rows
+    block = tile // present.shape[-1]
+    segments = []
+    for first_row in range(0, tile, block):
+        parts = 1 if first_row + block < tile else LAST
+        segments += [(first_row + i * (block // parts), block // parts) for i in range(parts)]
+    chunks = pair * len(segments)
     planes = col_devices // 4
     sends = 4 * planes - 1
-    relayed = (row_devices // 2, pair, tile // rows)
+    relayed = (row_devices // 2, pair, len(segments))
     return pl.pallas_call(
-        functools.partial(kernel, (row_devices, col_devices, chunks)),
+        functools.partial(kernel, (row_devices, col_devices, tuple(segments))),
         out_shape=jax.ShapeDtypeStruct(coeffs.shape, jnp.float32),
         in_specs=[pl.BlockSpec(memory_space=pltpu.SMEM)] * 2
-        + [pl.BlockSpec(memory_space=pltpu.VMEM)] * 2,
-        out_specs=pl.BlockSpec(memory_space=pltpu.VMEM),
-        scratch_shapes=[pltpu.VMEM((col_devices, rows, tile), jnp.float32) for _ in range(chunks)]
+        + [pl.BlockSpec(memory_space=pl.ANY)] * 2,
+        out_specs=pl.BlockSpec(memory_space=pl.ANY),
+        scratch_shapes=[
+            pltpu.VMEM((col_devices, segments[k // pair][1], tile), jnp.float32)
+            for k in range(chunks)
+        ]
         + [
             pltpu.VMEM((slots, tile, tile), jnp.bfloat16),
             pltpu.VMEM((slots, tile, tile), jnp.bfloat16),
             pltpu.VMEM((pair, tile, tile), jnp.float32),
             pltpu.VMEM((pair, tile, tile), jnp.float32),
-            pltpu.VMEM(relayed + (rows // 2, tile), jnp.float32),
-            pltpu.VMEM(relayed + (rows // 2, tile), jnp.float32),
+            pltpu.VMEM(relayed[:2] + (tile // 2, tile), jnp.float32),
+            pltpu.VMEM(relayed[:2] + (tile // 2, tile), jnp.float32),
             pltpu.SemaphoreType.DMA((chunks, sends)),
             pltpu.SemaphoreType.DMA((chunks, col_devices)),
-            pltpu.SemaphoreType.DMA((pair, tile // rows, 2)),
-            pltpu.SemaphoreType.DMA((pair, tile // rows, 2)),
+            pltpu.SemaphoreType.DMA((pair, len(segments), 2)),
+            pltpu.SemaphoreType.DMA((pair, len(segments), 2)),
             pltpu.SemaphoreType.DMA(relayed),
             pltpu.SemaphoreType.DMA(relayed),
             pltpu.SemaphoreType.DMA(relayed),
             pltpu.SemaphoreType.DMA(relayed),
+            pltpu.VMEM(coeffs.shape, jnp.float32),
+            pltpu.VMEM((slots, tile, tile), jnp.float32),
+            pltpu.VMEM(coeffs.shape, jnp.float32),
+            pltpu.SemaphoreType.DMA,
+            pltpu.SemaphoreType.DMA((slots,)),
+            pltpu.SemaphoreType.DMA((pair, tile // block)),
         ],
         compiler_params=pltpu.CompilerParams(
             collective_id=0, has_side_effects=True, vmem_limit_bytes=60 * 2**20),

time: 123 us -> 120 us (0.976)
  Pallas kernels: 120 us -> 117 us
    pallas_call x1, Pallas kernels: 120 us -> 117 us  [on_device(): pl.pallas_call(functools.partial(kernel, (row_devices, col_devices, tuple...]
where the time goes in v3:
time: 120 us
  Pallas kernels  117 us (98%)
  local copies, waits for them, and re-layouts  3.08 us (3%)
    pallas_call x1, Pallas kernels, on_device(): pl.pallas_call(functools.partial(kernel, (row_devices, col_devices, tuple...  117 us
    unnamed x1, local copies, waits for them, and re-layouts  3.08 us

profile of v3, /device:TPU:6, one launch (start us, length us, event | category | flops | bytes accessed | tf_op | source)
XLA Modules:
  0.0 119.8 jit_solution(7928963453384847586)
XLA Ops:
  0.0 116.7 %shard_map.46 = f32[1024,512]{1,0:T(8,128)} custom-call(s32[1,3]{1,0:T(1,128)} %source_ref.1, s32[1,4,4,4]{3,2,1,0:T(4,128)} %present_ref.1, f32[1024,512]{1,0:T(8,128)} %c_hbm.1, f32[1,4,512,512]{3,2,1,0:T(8,128)} %m_hbm.1), custom_call_target="tpu_custom_call" | custom-call | tf_op jit(solution)/shard_map/pallas_call | solution.py:289
  116.7 3.1 %copy.6 = f32[1024,512]{1,0:T(8,128)} copy(f32[1024,512]{1,0:T(8,128)} %shard_map.46) | data formatting | bytes 4194304

commit v4 on v3

--- a/solution.py
+++ b/solution.py
@@ -10,7 +10,7 @@
 MESH = pl.DeviceIdType.MESH
 AHEAD = 2
 DELAY = 1
-LAST = 2
+PARTS = 2
 
 
 def kernel(sizes, source_ref, present_ref, c_hbm, m_hbm, out_hbm, *scratch):
@@ -280,7 +280,7 @@
     block = tile // present.shape[-1]
     segments = []
     for first_row in range(0, tile, block):
-        parts = 1 if first_row + block < tile else LAST
+        parts = PARTS
         segments += [(first_row + i * (block // parts), block // parts) for i in range(parts)]
     chunks = pair * len(segments)
     planes = col_devices // 4

time: 120 us -> 119 us (level)
  Pallas kernels: 117 us -> 115 us
    pallas_call x1, Pallas kernels: 117 us -> 115 us  [on_device(): pl.pallas_call(functools.partial(kernel, (row_devices, col_devices, tuple...]
where the time goes in v4:
time: 119 us; the launch traced here: 118 us
  Pallas kernels  115 us (97%)
  local copies, waits for them, and re-layouts  3.08 us (3%)
    pallas_call x1, Pallas kernels, on_device(): pl.pallas_call(functools.partial(kernel, (row_devices, col_devices, tuple...  115 us
    unnamed x1, local copies, waits for them, and re-layouts  3.08 us

profile of v4, /device:TPU:6, one launch (start us, length us, event | category | flops | bytes accessed | tf_op | source)
XLA Modules:
  0.0 118.4 jit_solution(8081585920534143740)
XLA Ops:
  0.0 115.3 %shard_map.46 = f32[1024,512]{1,0:T(8,128)} custom-call(s32[1,3]{1,0:T(1,128)} %source_ref.1, s32[1,4,4,4]{3,2,1,0:T(4,128)} %present_ref.1, f32[1024,512]{1,0:T(8,128)} %c_hbm.1, f32[1,4,512,512]{3,2,1,0:T(8,128)} %m_hbm.1), custom_call_target="tpu_custom_call" | custom-call | tf_op jit(solution)/shard_map/pallas_call | solution.py:289
  115.3 3.1 %copy.6 = f32[1024,512]{1,0:T(8,128)} copy(f32[1024,512]{1,0:T(8,128)} %shard_map.46) | data formatting | bytes 4194304
